TPU v7x, 512 devices: a whole 4x4x16 slice. The times are simulated.
512 devices in a mesh: src: 16 (over y, x_lo, core), gz: 32 (over x_hi, z).
Axes of the slice: x: 4 (x_hi: 2, x_lo: 2; x = x_hi * 2 + x_lo), y: 4, z: 16, core: 2. Of those that a mesh axis runs over, the one named last changes fastest.
Arguments:
- conductivity: float32 [128, 128, 128], P('gz'), may hold values from 0.2 to 5
- perturbation: float32 [128, 128, 128], P('gz'), may hold values from -6 to 6
- fields: float32 [32, 128, 128, 128], P('src', 'gz'), may hold values from -6 to 6
- increment_start: float32 [32, 128, 128, 128], P('src', 'gz'), may hold values from -3 to 3
- adjoint_start: float32 [32, 128, 128, 128], P('src', 'gz'), may hold values from -0.625 to 0.625
- receivers: int32 [32, 512, 2], P('src'), may hold values from 0 to 2097151
- dipole_weight: float32 [32, 512], P('src'), may hold values from 0.5 to 2
Outputs:
- hessian_product: float32 [128, 128, 128], P('gz', 'src')
- increment: float32 [32, 128, 128, 128], P('src', 'gz')
All inputs are finite; a program needn't handle non-finite values.
Results may differ from a plain program's by a relative error of at most 0.0003.
Values sent between devices are 32-bit elements; how exact they have to be, the bound alone decides.
A program may use at most 64 MiB of HBM per device.

v0:
```python
import jax
import jax.numpy as jnp
from jax import lax
from jax.sharding import PartitionSpec as P

SWEEPS = 2


LEAKAGE = 0.5
RELAXATION = 0.8
REGULARIZE = 0.05


def with_halo(x, sides, width):
    for axis, dim in sides:
        size, length = (lax.axis_size(axis), x.shape[dim])
        up = [(i, (i + 1) % size) for i in range(size - 1)]
        down = [(j, i) for i, j in up]
        last = lax.slice_in_dim(x, length - width, length, axis=dim)
        initial = lax.slice_in_dim(x, 0, width, axis=dim)
        before = lax.ppermute(last, axis, up)
        after = lax.ppermute(initial, axis, down)
        x = jnp.concatenate([before, x, after], axis=dim)
    return x


def stencil_sides(array):
    widths = [(0, 0)] * (array.ndim - 2) + [(1, 1), (1, 1)]
    padded = jnp.pad(array, widths)
    center = padded[..., 1:-1, 1:-1, 1:-1]
    neighbours = [
        padded[..., 2:, 1:-1, 1:-1],
        padded[..., :-2, 1:-1, 1:-1],
        padded[..., 1:-1, 2:, 1:-1],
        padded[..., 1:-1, :-2, 1:-1],
        padded[..., 1:-1, 1:-1, 2:],
        padded[..., 1:-1, 1:-1, :-2],
    ]
    return (center, neighbours)


def operate(sigma_pad, field_pad):
    sig_center, sig_near = stencil_sides(sigma_pad)
    fld_center, fld_near = stencil_sides(field_pad)
    result = LEAKAGE * sig_center * fld_center
    for sig_other, fld_other in zip(sig_near, fld_near):
        result = result + 0.5 * (sig_center + sig_other) * (fld_center - fld_other)
    return result


def diagonal(sigma_pad):
    sig_center, sig_near = stencil_sides(sigma_pad)
    result = LEAKAGE * sig_center
    for sig_other in sig_near:
        result = result + 0.5 * (sig_center + sig_other)
    return result


def correlate(adjoint_pad, field_pad):
    adj_center, adj_near = stencil_sides(adjoint_pad)
    fld_center, fld_near = stencil_sides(field_pad)
    result = LEAKAGE * adj_center * fld_center
    for adj_other, fld_other in zip(adj_near, fld_near):
        result = result + 0.5 * (adj_center - adj_other) * (fld_center - fld_other)
    return result


def laplacian(pert_pad):
    center, neighbours = stencil_sides(pert_pad)
    result = center - neighbours[0]
    for other in neighbours[1:]:
        result = result + (center - other)
    return result


def build_adjoint_source(increment, receivers, dipole_weight, z_offset):
    sources, depth, width_x, width_y = increment.shape
    count = depth * width_x * width_y
    cells = increment.reshape(sources, count)
    local_index = receivers - z_offset * (width_x * width_y)
    inside = (local_index >= 0) & (local_index < count)
    safe_index = jnp.clip(local_index, 0, count - 1)
    picked = jnp.take_along_axis(cells, safe_index.reshape(sources, -1), axis=1)
    picked = jnp.where(inside, picked.reshape(safe_index.shape), 0.0)
    partial_read = picked[..., 0] - picked[..., 1]
    reading = dipole_weight * lax.psum(partial_read, "gz")
    source_rows = jnp.arange(sources)[:, None]
    adjoint_source = jnp.zeros((sources, count), jnp.float32)
    adjoint_source = adjoint_source.at[source_rows, safe_index[..., 0]].add(
        jnp.where(inside[..., 0], reading, 0.0)
    )
    adjoint_source = adjoint_source.at[source_rows, safe_index[..., 1]].add(
        jnp.where(inside[..., 1], -reading, 0.0)
    )
    return adjoint_source.reshape(increment.shape)


def on_device(
    conductivity, perturbation, fields, increment_start, adjoint_start, receivers, dipole_weight
):
    sources, depth, width_x, width_y = fields.shape
    z_offset = lax.axis_index("gz") * depth
    stacked = jnp.concatenate([fields, perturbation[None], conductivity[None]], axis=0)
    extended = with_halo(stacked, (("gz", 1),), 1)
    field_near = extended[:sources]
    pert_near = extended[sources]
    sig_pad = extended[sources + 1]
    diag_own = diagonal(sig_pad)
    source_term = -operate(pert_near, field_near)
    increment = increment_start
    for sweep_index in range(SWEEPS):
        padded = with_halo(increment, (("gz", 1),), 1)
        increment = increment + RELAXATION * (source_term - operate(sig_pad, padded)) / diag_own
    adjoint_source = build_adjoint_source(increment, receivers, dipole_weight, z_offset)
    adjoint = adjoint_start
    for sweep_index in range(SWEEPS):
        padded = with_halo(adjoint, (("gz", 1),), 1)
        adjoint = adjoint + RELAXATION * (adjoint_source - operate(sig_pad, padded)) / diag_own
    adjoint_pad = with_halo(adjoint, (("gz", 1),), 1)
    partial_corr = jnp.sum(correlate(adjoint_pad, field_near), axis=0)
    share_rows = width_x // lax.axis_size("src")
    row_start = lax.axis_index("src") * share_rows
    summed = lax.psum(partial_corr, "src")
    summed = lax.dynamic_slice_in_dim(summed, row_start, share_rows, 1)
    smoothing = lax.dynamic_slice_in_dim(laplacian(pert_near), row_start, share_rows, 1)
    return (-summed + REGULARIZE * smoothing, increment)


def solution(mesh):
    return jax.shard_map(
        on_device,
        mesh=mesh,
        in_specs=(
            P("gz", None, None),
            P("gz", None, None),
            P("src", "gz", None, None),
            P("src", "gz", None, None),
            P("src", "gz", None, None),
            P("src", None, None),
            P("src", None),
        ),
        out_specs=(P("gz", "src", None), P("src", "gz", None, None)),
        check_vma=False,
    )
```

profile of v0, /device:TPU:1, one launch (start us, length us, event | category | flops | bytes accessed | tf_op | source)
XLA Modules:
  0.0 341.7 jit_solution(9664283661630605566)
XLA Ops:
  8.5 1.3 collective-permute-start
  9.8 5.0 %collective-permute-start.1 = (f32[4,1,128,128]{3,2,1,0:T(8,128)S(1)}, f32[4,1,128,128]{3,2,1,0:T(8,128)S(1)}, u32[]{:S(2)}, u32[]{:S(2)}) collective-permute-start(f32[4,1,128,128]{3,2,1,0:T(8,128)S(1)} %get-tuple-element.25), channel_id=1, source_target_pairs={{0,1},{1,2},{2,3},{3,4},{4,5},{5,6},{6,7},{7,8},{8,9},{9,10},{10,1... | collective-permute-start | bytes 786440 | tf_op jit(solution)/shard_map/ppermute | solution.py:21
  15.5 1.3 collective-permute-start.2
  16.8 4.2 %collective-permute-start.3 = (f32[2,1,128,128]{3,2,1,0:T(8,128)S(1)}, f32[2,1,128,128]{3,2,1,0:T(8,128)S(1)}, u32[]{:S(2)}, u32[]{:S(2)}) collective-permute-start(f32[2,1,128,128]{3,2,1,0:T(8,128)S(1)} %get-tuple-element.39), channel_id=1, source_target_pairs={{0,1},{1,2},{2,3},{3,4},{4,5},{5,6},{6,7},{7,8},{8,9},{9,10},{10,1... | collective-permute-start | bytes 393224 | tf_op jit(solution)/shard_map/ppermute | solution.py:21
  26.5 4.2 %collective-permute-start.7 = (f32[2,1,128,128]{3,2,1,0:T(8,128)}, f32[2,1,128,128]{3,2,1,0:T(8,128)S(1)}, u32[]{:S(2)}, u32[]{:S(2)}) collective-permute-start(f32[2,1,128,128]{3,2,1,0:T(8,128)} %get-tuple-element.35), channel_id=1, source_target_pairs={{0,1},{1,2},{2,3},{3,4},{4,5},{5,6},{6,7},{7,8},{8,9},{9,10},{10,1... | collective-permute-start | bytes 393224 | tf_op jit(solution)/shard_map/ppermute | solution.py:21
  31.3 1.3 add_multiply_fusion.3
  34.6 1.4 fusion.87
  36.1 1.3 collective-permute-start.4
  37.4 5.4 %collective-permute-start.5 = (f32[2,1,128,128]{3,2,1,0:T(8,128)S(1)}, f32[2,1,128,128]{3,2,1,0:T(8,128)S(1)}, u32[]{:S(2)}, u32[]{:S(2)}) collective-permute-start(f32[2,1,128,128]{3,2,1,0:T(8,128)S(1)} %get-tuple-element.37), channel_id=1, source_target_pairs={{0,1},{1,2},{2,3},{3,4},{4,5},{5,6},{6,7},{7,8},{8,9},{9,10},{10,1... | collective-permute-start | bytes 393224 | tf_op jit(solution)/shard_map/ppermute | solution.py:21
  42.8 2.7 select_maximum_fusion.4
  48.0 17.7 %gather_fusion = f32[2048]{0:T(1024)S(1)} fusion(f32[2,65536]{1,0:T(2,128)S(1)} %bitcast.63, s32[2048]{0:T(1024)S(1)} %bitcast.64), kind=kCustom, calls=%fused_computation | custom fusion | bytes 32768 | tf_op jit(solution)/shard_map/jit(take_along_axis)/gather | solution.py:83
  66.4 68.9 %psum.14 = f32[2,512]{1,0:T(2,128)S(1)} all-reduce(f32[2,512]{1,0:T(2,128)S(1)} %bitcast.86), channel_id=1, replica_groups=mesh['src'=16,'gz'=32] {'gz'}, use_global_device_ids=true, to_apply=%region_0.1 | all-reduce | flops 1024 | bytes 8192 | tf_op jit(solution)/shard_map/psum | solution.py:86
  135.4 7.5 %scatter_custom_fusion = f32[131072]{0:T(1024)S(1)} fusion(s32[1024]{0:T(1024)S(1)} %bitcast.87, f32[1024]{0:T(1024)S(1)} %bitcast.88, f32[]{:T(128)} %constant.13.clone.1), kind=kCustom, calls=%fused_computation.191 | custom fusion | flops 1024 | bytes 524292
  143.0 7.7 %scatter_fusion = f32[131072]{0:T(1024)S(1)} fusion(f32[131072]{0:T(1024)S(1)} %scatter_custom_fusion, s32[1024]{0:T(1024)S(1)} %bitcast.84, f32[1024]{0:T(1024)S(1)} %bitcast.85), kind=kCustom, calls=%fused_computation.2 | custom fusion | flops 1024 | bytes 16384
  150.7 4.0 %fusion.51 = f32[2,4,128,128]{3,2,1,0:T(8,128)S(1)} fusion(f32[2,4,128,128]{3,2,1,0:T(8,128)} %param.11, f32[2,4,128,128]{3,2,1,0:T(8,128)S(1)} %bitcast.65, f32[2,6,130,130]{3,2,1,0:T(8,128)} %select_maximum_fusion.4, f32[2,1,128,128]{3,2,1,0:T(8,128)S(1)} %copy-done.22, f32[2,1,128,128]{3,2,1,0:T(8,128)} %collective-permute-done.6, ...), kind=kLoop, calls=%fused_computation.95 | loop fusion | flops 3276800 | bytes 6029312 | tf_op jit(solution)/shard_map/add | solution.py:118
  154.7 1.4 collective-permute-start.8
  156.1 4.0 %collective-permute-start.9 = (f32[2,1,128,128]{3,2,1,0:T(8,128)S(1)}, f32[2,1,128,128]{3,2,1,0:T(8,128)S(1)}, u32[]{:S(2)}, u32[]{:S(2)}) collective-permute-start(f32[2,1,128,128]{3,2,1,0:T(8,128)S(1)} %get-tuple-element.33), channel_id=1, source_target_pairs={{0,1},{1,2},{2,3},{3,4},{4,5},{5,6},{6,7},{7,8},{8,9},{9,10},{10,1... | collective-permute-start | bytes 393224 | tf_op jit(solution)/shard_map/ppermute | solution.py:21
  160.5 1.5 collective-permute-done.9
  163.3 1.3 collective-permute-start.10
  164.6 4.4 %collective-permute-start.11 = (f32[2,1,128,128]{3,2,1,0:T(8,128)S(1)}, f32[2,1,128,128]{3,2,1,0:T(8,128)S(1)}, u32[]{:S(2)}, u32[]{:S(2)}) collective-permute-start(f32[2,1,128,128]{3,2,1,0:T(8,128)S(1)} %get-tuple-element.31), channel_id=1, source_target_pairs={{0,1},{1,2},{2,3},{3,4},{4,5},{5,6},{6,7},{7,8},{8,9},{9,10},{10,1... | collective-permute-start | bytes 393224 | tf_op jit(solution)/shard_map/ppermute | solution.py:21
  169.5 1.5 collective-permute-done.11
  171.5 1.7 fusion.10
  173.2 160.2 %all-reduce.10.cloned.1.call-done = f32[4,128,128]{2,1,0:T(8,128)} async-done(((f32[4,128,128]{2,1,0:T(8,128)}), f32[4,128,128]{2,1,0:T(8,128)}) %all-reduce.10.cloned.1.call-update) | async-done | bytes 262160 | tf_op jit(solution)/shard_map/psum | solution.py:123
  333.4 1.4 fusion.118
  (104 shorter events, 15.6 us)
Async XLA Ops:
  7.2 13.8 %copy-start.16 = (f32[2,4,128,128]{3,2,1,0:T(8,128)S(1)}, f32[2,4,128,128]{3,2,1,0:T(8,128)}, u32[]{:S(2)}) copy-start(f32[2,4,128,128]{3,2,1,0:T(8,128)} %param.11) | copy-start | bytes 1572868
  7.2 15.8 %copy-start.23 = (s32[2,512,2]{1,2,0:T(2,128)S(1)}, s32[2,512,2]{1,2,0:T(2,128)}, u32[]{:S(2)}) copy-start(s32[2,512,2]{1,2,0:T(2,128)} %param.12) | copy-start | bytes 24580
  7.2 326.2 %all-reduce.10.cloned.1.call-start = ((), (), s32[]{:S(2)}) async-start(), calls=%async_computation | async-start | bytes 524288 | tf_op jit(solution)/shard_map/psum | solution.py:123
  8.5 22.7 %collective-permute-start = (f32[4,1,128,128]{3,2,1,0:T(8,128)S(1)}, f32[4,1,128,128]{3,2,1,0:T(8,128)S(1)}, u32[]{:S(2)}, u32[]{:S(2)}) collective-permute-start(f32[4,1,128,128]{3,2,1,0:T(8,128)S(1)} %get-tuple-element.26), channel_id=1, source_target_pairs={{1,0},{2,1},{3,2},{4,3},{5,4},{6,5},{7,6},{8,7},{9,8},{10,9},{11,1... | collective-permute-start | bytes 786440 | tf_op jit(solution)/shard_map/ppermute | solution.py:22
  9.8 21.4 %collective-permute-start.1 = (f32[4,1,128,128]{3,2,1,0:T(8,128)S(1)}, f32[4,1,128,128]{3,2,1,0:T(8,128)S(1)}, u32[]{:S(2)}, u32[]{:S(2)}) collective-permute-start(f32[4,1,128,128]{3,2,1,0:T(8,128)S(1)} %get-tuple-element.25), channel_id=1, source_target_pairs={{0,1},{1,2},{2,3},{3,4},{4,5},{5,6},{6,7},{7,8},{8,9},{9,10},{10,1... | collective-permute-start | bytes 786440 | tf_op jit(solution)/shard_map/ppermute | solution.py:21
  15.5 11.0 %collective-permute-start.2 = (f32[2,1,128,128]{3,2,1,0:T(8,128)}, f32[2,1,128,128]{3,2,1,0:T(8,128)S(1)}, u32[]{:S(2)}, u32[]{:S(2)}) collective-permute-start(f32[2,1,128,128]{3,2,1,0:T(8,128)} %get-tuple-element.40), channel_id=1, source_target_pairs={{1,0},{2,1},{3,2},{4,3},{5,4},{6,5},{7,6},{8,7},{9,8},{10,9},{11,1... | collective-permute-start | bytes 393224 | tf_op jit(solution)/shard_map/ppermute | solution.py:22
  16.8 13.9 %collective-permute-start.3 = (f32[2,1,128,128]{3,2,1,0:T(8,128)S(1)}, f32[2,1,128,128]{3,2,1,0:T(8,128)S(1)}, u32[]{:S(2)}, u32[]{:S(2)}) collective-permute-start(f32[2,1,128,128]{3,2,1,0:T(8,128)S(1)} %get-tuple-element.39), channel_id=1, source_target_pairs={{0,1},{1,2},{2,3},{3,4},{4,5},{5,6},{6,7},{7,8},{8,9},{9,10},{10,1... | collective-permute-start | bytes 393224 | tf_op jit(solution)/shard_map/ppermute | solution.py:21
  21.7 21.1 %collective-permute-start.6 = (f32[2,1,128,128]{3,2,1,0:T(8,128)}, f32[2,1,128,128]{3,2,1,0:T(8,128)}, u32[]{:S(2)}, u32[]{:S(2)}) collective-permute-start(f32[2,1,128,128]{3,2,1,0:T(8,128)} %get-tuple-element.36), channel_id=1, source_target_pairs={{1,0},{2,1},{3,2},{4,3},{5,4},{6,5},{7,6},{8,7},{9,8},{10,9},{11,1... | collective-permute-start | bytes 393224 | tf_op jit(solution)/shard_map/ppermute | solution.py:22
  26.5 16.3 %collective-permute-start.7 = (f32[2,1,128,128]{3,2,1,0:T(8,128)}, f32[2,1,128,128]{3,2,1,0:T(8,128)S(1)}, u32[]{:S(2)}, u32[]{:S(2)}) collective-permute-start(f32[2,1,128,128]{3,2,1,0:T(8,128)} %get-tuple-element.35), channel_id=1, source_target_pairs={{0,1},{1,2},{2,3},{3,4},{4,5},{5,6},{6,7},{7,8},{8,9},{9,10},{10,1... | collective-permute-start | bytes 393224 | tf_op jit(solution)/shard_map/ppermute | solution.py:21
  34.0 12.1 %copy-start.3 = (f32[4,128,128]{2,1,0:T(8,128)}, f32[4,128,128]{2,1,0:T(8,128)S(1)}, u32[]{:S(2)}) copy-start(f32[4,128,128]{2,1,0:T(8,128)S(1)} %get-tuple-element.12) | copy-start | bytes 786436
  34.0 12.1 %copy-start.5 = (f32[4,128,128]{2,1,0:T(8,128)}, f32[4,128,128]{2,1,0:T(8,128)S(1)}, u32[]{:S(2)}) copy-start(f32[4,128,128]{2,1,0:T(8,128)S(1)} %get-tuple-element.13) | copy-start | bytes 786436
  34.0 12.1 %copy-start.7 = (f32[4,128,128]{2,1,0:T(8,128)}, f32[4,128,128]{2,1,0:T(8,128)S(1)}, u32[]{:S(2)}) copy-start(f32[4,128,128]{2,1,0:T(8,128)S(1)} %get-tuple-element.14) | copy-start | bytes 786436
  34.0 12.1 %copy-start.9 = (f32[4,128,128]{2,1,0:T(8,128)}, f32[4,128,128]{2,1,0:T(8,128)S(1)}, u32[]{:S(2)}) copy-start(f32[4,128,128]{2,1,0:T(8,128)S(1)} %get-tuple-element.15) | copy-start | bytes 786436
  34.0 12.1 %copy-start.11 = (f32[4,128,128]{2,1,0:T(8,128)}, f32[4,128,128]{2,1,0:T(8,128)S(1)}, u32[]{:S(2)}) copy-start(f32[4,128,128]{2,1,0:T(8,128)S(1)} %get-tuple-element.16) | copy-start | bytes 786436
  34.0 12.1 %copy-start.13 = (f32[4,128,128]{2,1,0:T(8,128)}, f32[4,128,128]{2,1,0:T(8,128)S(1)}, u32[]{:S(2)}) copy-start(f32[4,128,128]{2,1,0:T(8,128)S(1)} %get-tuple-element.46) | copy-start | bytes 786436
  34.6 8.2 %copy-start.17 = (f32[2,4,128,128]{3,2,1,0:T(8,128)S(1)}, f32[2,4,128,128]{3,2,1,0:T(8,128)}, u32[]{:S(2)}) copy-start(f32[2,4,128,128]{3,2,1,0:T(8,128)} %param.11) | copy-start | bytes 1572868
  36.1 9.4 %collective-permute-start.4 = (f32[2,1,128,128]{3,2,1,0:T(8,128)S(1)}, f32[2,1,128,128]{3,2,1,0:T(8,128)S(1)}, u32[]{:S(2)}, u32[]{:S(2)}) collective-permute-start(f32[2,1,128,128]{3,2,1,0:T(8,128)S(1)} %get-tuple-element.38), channel_id=1, source_target_pairs={{1,0},{2,1},{3,2},{4,3},{5,4},{6,5},{7,6},{8,7},{9,8},{10,9},{11,1... | collective-permute-start | bytes 393224 | tf_op jit(solution)/shard_map/ppermute | solution.py:22
  37.4 8.1 %collective-permute-start.5 = (f32[2,1,128,128]{3,2,1,0:T(8,128)S(1)}, f32[2,1,128,128]{3,2,1,0:T(8,128)S(1)}, u32[]{:S(2)}, u32[]{:S(2)}) collective-permute-start(f32[2,1,128,128]{3,2,1,0:T(8,128)S(1)} %get-tuple-element.37), channel_id=1, source_target_pairs={{0,1},{1,2},{2,3},{3,4},{4,5},{5,6},{6,7},{7,8},{8,9},{9,10},{10,1... | collective-permute-start | bytes 393224 | tf_op jit(solution)/shard_map/ppermute | solution.py:21
  48.0 18.4 %copy-start.24 = (s32[2,512,2]{1,2,0:T(2,128)S(1)}, s32[2,512,2]{1,2,0:T(2,128)}, u32[]{:S(2)}) copy-start(s32[2,512,2]{1,2,0:T(2,128)} %param.12) | copy-start | bytes 24580
  48.0 87.4 %copy-start.25 = (f32[2,512]{1,0:T(2,128)S(1)}, f32[2,512]{1,0:T(2,128)}, u32[]{:S(2)}) copy-start(f32[2,512]{1,0:T(2,128)} %param.13) | copy-start | bytes 12292
  154.7 5.8 %collective-permute-start.8 = (f32[2,1,128,128]{3,2,1,0:T(8,128)S(1)}, f32[2,1,128,128]{3,2,1,0:T(8,128)S(1)}, u32[]{:S(2)}, u32[]{:S(2)}) collective-permute-start(f32[2,1,128,128]{3,2,1,0:T(8,128)S(1)} %get-tuple-element.34), channel_id=1, source_target_pairs={{1,0},{2,1},{3,2},{4,3},{5,4},{6,5},{7,6},{8,7},{9,8},{10,9},{11,1... | collective-permute-start | bytes 393224 | tf_op jit(solution)/shard_map/ppermute | solution.py:22
  156.1 5.9 %collective-permute-start.9 = (f32[2,1,128,128]{3,2,1,0:T(8,128)S(1)}, f32[2,1,128,128]{3,2,1,0:T(8,128)S(1)}, u32[]{:S(2)}, u32[]{:S(2)}) collective-permute-start(f32[2,1,128,128]{3,2,1,0:T(8,128)S(1)} %get-tuple-element.33), channel_id=1, source_target_pairs={{0,1},{1,2},{2,3},{3,4},{4,5},{5,6},{6,7},{7,8},{8,9},{9,10},{10,1... | collective-permute-start | bytes 393224 | tf_op jit(solution)/shard_map/ppermute | solution.py:21
  163.3 6.1 %collective-permute-start.10 = (f32[2,1,128,128]{3,2,1,0:T(8,128)S(1)}, f32[2,1,128,128]{3,2,1,0:T(8,128)S(1)}, u32[]{:S(2)}, u32[]{:S(2)}) collective-permute-start(f32[2,1,128,128]{3,2,1,0:T(8,128)S(1)} %get-tuple-element.32), channel_id=1, source_target_pairs={{1,0},{2,1},{3,2},{4,3},{5,4},{6,5},{7,6},{8,7},{9,8},{10,9},{11,1... | collective-permute-start | bytes 393224 | tf_op jit(solution)/shard_map/ppermute | solution.py:22
  164.6 6.3 %collective-permute-start.11 = (f32[2,1,128,128]{3,2,1,0:T(8,128)S(1)}, f32[2,1,128,128]{3,2,1,0:T(8,128)S(1)}, u32[]{:S(2)}, u32[]{:S(2)}) collective-permute-start(f32[2,1,128,128]{3,2,1,0:T(8,128)S(1)} %get-tuple-element.31), channel_id=1, source_target_pairs={{0,1},{1,2},{2,3},{3,4},{4,5},{5,6},{6,7},{7,8},{8,9},{9,10},{10,1... | collective-permute-start | bytes 393224 | tf_op jit(solution)/shard_map/ppermute | solution.py:21
  (15 other events, 92.6 us)
Sparse Core Ops, SparseCore 0:
  173.3 160.0 all-reduce.9
where the time goes:
time: 342 us
  waiting for transfers between devices  164 us (48%)
  blocking collectives  68.9 us (20%)
  other arithmetic  35.9 us (10%)
  starting transfers between devices  35 us (10%)
  local copies, waits for them, and re-layouts  22.9 us (7%)
  between operations  14.8 us (4%)
    psum x1, waiting for transfers between devices, on_device(): summed = lax.psum(partial_corr, 'src')  160 us
    psum x1, blocking collectives, build_adjoint_source(): reading = dipole_weight * lax.psum(partial_read, 'gz')  68.9 us
    ppermute x6, starting transfers between devices, with_halo(): before = lax.ppermute(last, axis, up)  27.1 us
    gather x3, local copies, waits for them, and re-layouts, build_adjoint_source(): picked = jnp.take_along_axis(cells, safe_index.reshape(sources, -1), axis=1)  18.3 us
    unnamed x7, other arithmetic  17.5 us
    ppermute x6, starting transfers between devices, with_halo(): after = lax.ppermute(initial, axis, down)  7.86 us
  transfers between devices with their start and end apart: 13, of which 5 were waited for; matrix products, arithmetic and copies ran while one was open for 4% of the time, Pallas kernels for 0%

commit v1 on v0

v1 whole, which is shorter than its diff:
```python
import functools

import jax
import jax.numpy as jnp
from jax import lax
from jax.experimental import pallas as pl
from jax.experimental.pallas import tpu as pltpu
from jax.sharding import PartitionSpec as P

LEAKAGE = 0.5
RELAXATION = 0.8
REGULARIZE = 0.05
KEEP = 1.0 - RELAXATION
MESH = pl.DeviceIdType.MESH
DMA = pltpu.SemaphoreType.DMA
QUARTER = 4


def ahead(plane, axis):
    return pltpu.roll(plane, plane.shape[axis] - 1, axis)


def behind(plane, axis):
    return pltpu.roll(plane, 1, axis)


def kernel(
    sigma_hbm, pert_hbm, field_hbm, start_hbm, adjoint_hbm, cells_ref, weight_ref,
    hess_ref, inc_hbm,
    sg, pe, fe, ie, i1, o2, ae, a1, a2, b1,
    coef, ew, nb, st, vh, ns, lap,
    hot, spot, read, got_a, part, got_b, co, rb,
    in_sem, out_sem, z_send, z_recv, a_send, a_recv, b_send, b_recv, s_send, s_recv,
):
    src, gz = lax.axis_index("src"), lax.axis_index("gz")
    n_src, n_gz = lax.axis_size("src"), lax.axis_size("gz")
    sources, depth, nx, ny = field_hbm.shape
    dipoles = weight_ref.shape[1]
    has_lo, has_hi = gz > 0, gz < n_gz - 1
    row = lax.broadcasted_iota(jnp.int32, (nx, ny), 0)
    col = lax.broadcasted_iota(jnp.int32, (nx, ny), 1)
    inside = {(0, 1): row < nx - 1, (0, -1): row > 0, (1, 1): col < ny - 1, (1, -1): col > 0}
    sides = tuple(inside)

    def shifted(plane, side):
        return ahead(plane, side[0]) if side[1] > 0 else behind(plane, side[0])

    def neighbour(plane, side):
        return jnp.where(inside[side], shifted(plane, side), 0.0)

    lo, hi = (src, gz - 1), (src, gz + 1)
    half = n_gz // 2
    x_part, z_part = gz // half, lax.rem(gz, half)
    z_group, z_in = z_part // QUARTER, lax.rem(z_part, QUARTER)
    groups = half // QUARTER
    near = []
    for dx in range(2):
        for dz in range(QUARTER):
            if dx or dz:
                near.append((src, lax.rem(x_part + dx, 2) * half + z_group * QUARTER + lax.rem(z_in + dz, QUARTER)))
    far = [(src, x_part * half + lax.rem(z_group + d, groups) * QUARTER + z_in) for d in range(1, groups)]
    mates = [(lax.rem(src + d, n_src), gz) for d in range(1, n_src)]

    barrier = pltpu.get_barrier_semaphore()

    def signal(device):
        pl.semaphore_signal(barrier, inc=1, device_id=device, device_id_type=MESH)

    pl.when(has_lo)(lambda: signal(lo))
    pl.when(has_hi)(lambda: signal(hi))
    for device in near + far + mates:
        signal(device)

    loads = [
        pltpu.make_async_copy(sigma_hbm, sg.at[pl.ds(3, depth)], in_sem.at[0]),
        pltpu.make_async_copy(pert_hbm, pe.at[pl.ds(1, depth)], in_sem.at[1]),
        pltpu.make_async_copy(start_hbm, ie.at[:, pl.ds(1, depth)], in_sem.at[2]),
        pltpu.make_async_copy(field_hbm, fe.at[:, pl.ds(1, depth)], in_sem.at[3]),
        pltpu.make_async_copy(adjoint_hbm, ae.at[:, pl.ds(3, depth)], in_sem.at[4]),
    ]
    for load in loads:
        load.start()

    empty = jnp.zeros((nx, ny), jnp.float32)

    def clear(high):
        for i in range(3):
            sg[depth + 3 + i if high else i] = empty
            for s in range(sources):
                ae[s, depth + 3 + i if high else i] = empty
        e = depth + 1 if high else 0
        pe[e] = empty
        for s in range(sources):
            fe[s, e] = empty
            ie[s, e] = empty
            vh[1 if high else 0, s] = empty

    pl.when(jnp.logical_not(has_lo))(lambda: clear(False))
    pl.when(jnp.logical_not(has_hi))(lambda: clear(True))

    def edge(index, up_src, up_dst, down_src, down_dst):
        up = pltpu.make_async_remote_copy(
            src_ref=up_src, dst_ref=up_dst, send_sem=z_send.at[0, index], recv_sem=z_recv.at[0, index],
            device_id=hi, device_id_type=MESH)
        down = pltpu.make_async_remote_copy(
            src_ref=down_src, dst_ref=down_dst, send_sem=z_send.at[1, index], recv_sem=z_recv.at[1, index],
            device_id=lo, device_id_type=MESH)
        return up, down

    def begin(pair):
        pl.when(has_hi)(pair[0].start)
        pl.when(has_lo)(pair[1].start)

    def sent(pair):
        pl.when(has_hi)(pair[0].wait_send)
        pl.when(has_lo)(pair[1].wait_send)

    def arrived(pair):
        pl.when(has_lo)(pair[0].wait_recv)
        pl.when(has_hi)(pair[1].wait_recv)

    edge_sigma = edge(0, sg.at[pl.ds(depth, 3)], sg.at[pl.ds(0, 3)], sg.at[pl.ds(3, 3)], sg.at[pl.ds(depth + 3, 3)])
    edge_pert = edge(1, pe.at[depth], pe.at[0], pe.at[1], pe.at[depth + 1])
    edge_start = edge(2, ie.at[:, depth], ie.at[:, 0], ie.at[:, 1], ie.at[:, depth + 1])
    edge_field = edge(3, fe.at[:, depth], fe.at[:, 0], fe.at[:, 1], fe.at[:, depth + 1])
    edge_value = edge(4, nb.at[:, depth - 1], vh.at[0], nb.at[:, 0], vh.at[1])
    edge_adj = edge(5, ae.at[:, pl.ds(depth, 3)], ae.at[:, pl.ds(0, 3)], ae.at[:, pl.ds(3, 3)], ae.at[:, pl.ds(depth + 3, 3)])

    for load in loads:
        load.wait()
    pl.semaphore_wait(barrier, len(near) + len(far) + len(mates) + has_lo.astype(jnp.int32) + has_hi.astype(jnp.int32))

    begin(edge_sigma)
    begin(edge_pert)
    begin(edge_start)
    begin(edge_field)

    def local(k, carry):
        below, above = jnp.maximum(k - 1, 0), jnp.minimum(k + 1, depth - 1)
        has_below, has_above = (k > 0).astype(jnp.float32), (k < depth - 1).astype(jnp.float32)
        sig, pert = sg[k + 3], pe[k + 1]
        sig_z = [has_below * 0.5 * (sig + sg[below + 3]), has_above * 0.5 * (sig + sg[above + 3])]
        pert_z = [has_below * 0.5 * (pert + pe[below + 1]), has_above * 0.5 * (pert + pe[above + 1])]
        near_pert = [neighbour(pert, side) for side in sides]
        sig_w = [jnp.where(inside[side], 0.5 * (sig + shifted(sig, side)), 0.0) for side in sides]
        pert_w = [jnp.where(inside[side], 0.5 * (pert + other), 0.0) for side, other in zip(sides, near_pert)]
        pert_sum = (near_pert[0] + near_pert[1]) + (near_pert[2] + near_pert[3])
        diag = LEAKAGE * pert + 2.0 * pert + 0.5 * pert_sum + pert_z[0] + pert_z[1]
        for s in range(sources):
            field, start = fe[s, k + 1], ie[s, k + 1]
            term = pert_z[0] * fe[s, below + 1] + pert_z[1] * fe[s, above + 1] - diag * field
            near_field = empty
            for side, weight in zip(sides, pert_w):
                other = neighbour(field, side)
                term = term + weight * other
                near_field = near_field + other
            st[s, k] = term
            ns[s, k] = near_field
            total = term + sig_z[0] * ie[s, below + 1] + sig_z[1] * ie[s, above + 1]
            for side, weight in zip(sides, sig_w):
                total = total + weight * shifted(start, side)
            nb[s, k] = total
        lap[:, k] = (4.0 * pert - pert_sum).reshape(n_src, nx // n_src, ny)
        return carry

    lax.fori_loop(0, depth, local, 0)
    begin(edge_value)

    def electrodes(s):
        both = cells_ref[s]
        flat = jnp.concatenate([both[0:1], both[1:2]], axis=1)
        plane_row = flat // ny
        return plane_row - (gz * depth - 2) * nx, flat - plane_row * ny

    def mark(s):
        rows, columns = electrodes(s)
        spot_s = jnp.broadcast_to(columns, (ny, 2 * dipoles)) == lax.broadcasted_iota(jnp.int32, (ny, 2 * dipoles), 0)
        spot_s = jnp.where(spot_s, 1.0, 0.0).astype(jnp.bfloat16)
        for piece in range(3):
            spot[s, pl.ds(piece * ny, ny)] = spot_s

        def chunk(c, carry):
            index = lax.broadcasted_iota(jnp.int32, (nx, 2 * dipoles), 0) + c * nx
            match = jnp.broadcast_to(rows, (nx, 2 * dipoles)) == index
            hot[s, pl.ds(pl.multiple_of(c * nx, nx), nx)] = jnp.where(match, 1.0, 0.0).astype(jnp.bfloat16)
            return carry

        lax.fori_loop(0, depth + 4, chunk, 0)

    for s in range(sources):
        mark(s)

    arrived(edge_sigma)

    def coefficients(e, carry):
        sig, below, above = sg[e + 1], sg[e], sg[e + 2]
        others = [neighbour(sig, side) for side in sides]
        diag = (LEAKAGE + 3.0) * sig + 0.5 * (((others[0] + others[1]) + (others[2] + others[3])) + (below + above))
        plane = gz * depth + e - 2
        exists = jnp.logical_and(plane >= 0, plane < n_gz * depth)
        scale = jnp.where(exists, RELAXATION / diag, 0.0)
        ew[e] = scale
        scale = 0.5 * scale
        for i, side in enumerate(sides):
            coef[i, e] = jnp.where(inside[side], scale * (sig + others[i]), 0.0)
        coef[4, e] = scale * (sig + below)
        coef[5, e] = scale * (sig + above)
        return carry

    lax.fori_loop(0, depth + 4, coefficients, 0)

    def around(e, values, s, offset):
        v = e - offset
        center = values[s, v]
        total = coef[4, e] * values[s, v - 1] + coef[5, e] * values[s, v + 1]
        for i, side in enumerate(sides):
            total = total + coef[i, e] * shifted(center, side)
        return center, total

    sent(edge_sigma)
    sent(edge_pert)
    sent(edge_start)
    sent(edge_field)
    sent(edge_value)
    begin(edge_adj)
    arrived(edge_pert)
    arrived(edge_start)
    arrived(edge_field)
    arrived(edge_value)

    for k in range(1, depth - 1):
        for s in range(sources):
            i1[s, k + 1] = KEEP * ie[s, k + 1] + ew[k + 2] * nb[s, k]
    for own, other, v in ((0, -1, 0), (depth - 1, depth, 1)):
        sig_w = 0.5 * (sg[own + 3] + sg[other + 3])
        pert_w = 0.5 * (pe[own + 1] + pe[other + 1])
        lap[:, own] = lap[:, own] + (pe[own + 1] - pe[other + 1]).reshape(n_src, nx // n_src, ny)
        for s in range(sources):
            face = pert_w * (fe[s, other + 1] - fe[s, own + 1])
            st[s, own] = st[s, own] + face
            i1[s, own + 1] = KEEP * ie[s, own + 1] + ew[own + 2] * (nb[s, own] + face + sig_w * ie[s, other + 1])
            i1[s, other + 1] = KEEP * ie[s, other + 1] + ew[other + 2] * (vh[v, s] - face + sig_w * ie[s, own + 1])
    for k in range(depth - 1):
        face = (pe[k + 1] - pe[k + 2]).reshape(n_src, nx // n_src, ny)
        lap[:, k] = lap[:, k] + face
        lap[:, k + 1] = lap[:, k + 1] - face

    def second(k, carry):
        for s in range(sources):
            center, total = around(k + 2, i1, s, 1)
            o2[s, k] = KEEP * center + ew[k + 2] * st[s, k] + total
        return carry

    lax.fori_loop(0, depth, second, 0)
    store = pltpu.make_async_copy(o2, inc_hbm, out_sem)
    store.start()

    def pick(s):
        rows, _ = electrodes(s)
        value = o2[s].reshape(depth * nx, ny)
        high = value.astype(jnp.bfloat16)
        rest = value - high.astype(jnp.float32)
        middle = rest.astype(jnp.bfloat16)
        low = (rest - middle.astype(jnp.float32)).astype(jnp.bfloat16)
        columns = jnp.dot(
            jnp.concatenate([high, middle, low], axis=1), spot[s], preferred_element_type=jnp.float32)
        index = lax.broadcasted_iota(jnp.int32, columns.shape, 0) + 2 * nx
        picked = jnp.sum(jnp.where(jnp.broadcast_to(rows, columns.shape) == index, columns, 0.0), axis=0, keepdims=True)
        reading = picked[:, :dipoles] - picked[:, dipoles:]
        for i in range(dipoles // 128):
            read[pl.ds(s * (dipoles // 128) + i, 1)] = reading[:, i * 128:(i + 1) * 128]

    for s in range(sources):
        pick(s)

    def spread(devices, source, target, send, recv):
        copies = []
        for i, device in enumerate(devices):
            copies.append(pltpu.make_async_remote_copy(
                src_ref=source(i), dst_ref=target.at[i], send_sem=send.at[i], recv_sem=recv.at[i],
                device_id=device, device_id_type=MESH))
            copies[-1].start()
        return copies

    near_copies = spread(near, lambda i: read, got_a, a_send, a_recv)

    def across(k, carry):
        for s in range(sources):
            ns[s, k] = ns[s, k] + (fe[s, k] + fe[s, k + 2])
        return carry

    lax.fori_loop(0, depth, across, 0)

    total = read[...]
    for i, copy in enumerate(near_copies):
        copy.wait_recv()
        total = total + got_a[i]
    part[...] = total
    far_copies = spread(far, lambda i: part, got_b, b_send, b_recv)

    arrived(edge_adj)

    def adjoint_first(e, carry):
        for s in range(sources):
            center, total = around(e, ae, s, -1)
            a1[s, e] = KEEP * center + total
        return carry

    lax.fori_loop(0, depth + 4, adjoint_first, 0)

    def adjoint_second(e, carry):
        for s in range(sources):
            center, total = around(e, a1, s, 0)
            a2[s, e - 1] = KEEP * center + total
        return carry

    lax.fori_loop(1, depth + 3, adjoint_second, 0)

    total = part[...]
    for i, copy in enumerate(far_copies):
        copy.wait_recv()
        total = total + got_b[i]
    for copy in near_copies + far_copies:
        copy.wait_send()
    read[...] = total

    def scatter(s):
        per = dipoles // 128
        value = jnp.concatenate([read[pl.ds(s * per + i, 1)] for i in range(per)], axis=1) * weight_ref[pl.ds(s, 1)]
        value = jnp.concatenate([value, -value], axis=1)
        high = value.astype(jnp.bfloat16)
        low = (value - high.astype(jnp.float32)).astype(jnp.bfloat16)
        pieces = jnp.concatenate([spot[s, pl.ds(0, ny)] * high, spot[s, pl.ds(0, ny)] * low], axis=0)
        placed = lax.dot_general(hot[s], pieces, (((1,), (1,)), ((), ())), preferred_element_type=jnp.float32)
        placed = (placed[:, :ny] + placed[:, ny:]).reshape(depth + 4, nx, ny)
        b1[s] = ew[...] * placed

    for s in range(sources):
        scatter(s)

    def adjoint_readings(e, carry):
        for s in range(sources):
            center, total = around(e, b1, s, 0)
            a2[s, e - 1] = a2[s, e - 1] + (1.0 + KEEP) * center + total
        return carry

    lax.fori_loop(1, depth + 3, adjoint_readings, 0)

    def correlate(k, carry):
        product = empty
        mixed = empty
        for s in range(sources):
            adj, field = a2[s, k + 1], fe[s, k + 1]
            near_adj = a2[s, k] + a2[s, k + 2]
            for side in sides:
                near_adj = near_adj + neighbour(adj, side)
            product = product + adj * field
            mixed = mixed + (adj * ns[s, k] + field * near_adj)
            mixed = mixed - (a2[s, k] * fe[s, k] + a2[s, k + 2] * fe[s, k + 2])
        around_product = empty
        for side in sides:
            around_product = around_product + neighbour(product, side)
        result = (LEAKAGE + 3.0) * product + 0.5 * (around_product - mixed)
        co[:, k] = result.reshape(n_src, nx // n_src, ny)
        return carry

    lax.fori_loop(0, depth, correlate, 0)

    mate_copies = spread(mates, lambda i: co.at[mates[i][0]], rb, s_send, s_recv)
    total = co[src]
    for i, copy in enumerate(mate_copies):
        copy.wait_recv()
        total = total + rb[i]
    hess_ref[...] = REGULARIZE * lap[src] - total

    sent(edge_adj)
    for copy in mate_copies:
        copy.wait_send()
    store.wait()


def on_device(conductivity, perturbation, fields, increment_start, adjoint_start, receivers, dipole_weight):
    sources, depth, nx, ny = fields.shape
    dipoles = dipole_weight.shape[1]
    n_src, n_gz = lax.axis_size("src"), lax.axis_size("gz")
    share = nx // n_src
    rows = sources * dipoles // 128

    def planes(*lead):
        return pltpu.VMEM((*lead, nx, ny), jnp.float32)

    near, far, mates = 2 * QUARTER - 1, n_gz // 2 // QUARTER - 1, n_src - 1
    scratch = [
        planes(depth + 6), planes(depth + 2), planes(sources, depth + 2), planes(sources, depth + 2),
        planes(sources, depth + 2), planes(sources, depth), planes(sources, depth + 6), planes(sources, depth + 4),
        planes(sources, depth + 2), planes(sources, depth + 4),
        planes(6, depth + 4), planes(depth + 4), planes(sources, depth), planes(sources, depth),
        planes(2, sources), planes(sources, depth), pltpu.VMEM((n_src, depth, share, ny), jnp.float32),
        pltpu.VMEM((sources, (depth + 4) * nx, 2 * dipoles), jnp.bfloat16),
        pltpu.VMEM((sources, 3 * ny, 2 * dipoles), jnp.bfloat16),
        pltpu.VMEM((rows, 128), jnp.float32), pltpu.VMEM((near, rows, 128), jnp.float32),
        pltpu.VMEM((rows, 128), jnp.float32), pltpu.VMEM((far, rows, 128), jnp.float32),
        pltpu.VMEM((n_src, depth, share, ny), jnp.float32), pltpu.VMEM((mates, depth, share, ny), jnp.float32),
        DMA((5,)), DMA, DMA((2, 6)), DMA((2, 6)), DMA((near,)), DMA((near,)), DMA((far,)), DMA((far,)),
        DMA((mates,)), DMA((mates,)),
    ]
    anywhere = pl.BlockSpec(memory_space=pl.ANY)
    vmem = pl.BlockSpec(memory_space=pltpu.VMEM)
    return pl.pallas_call(
        kernel,
        out_shape=(
            jax.ShapeDtypeStruct((depth, share, ny), jnp.float32),
            jax.ShapeDtypeStruct(increment_start.shape, jnp.float32),
        ),
        in_specs=[anywhere] * 5 + [vmem] * 2,
        out_specs=(vmem, anywhere),
        scratch_shapes=scratch,
        compiler_params=pltpu.CompilerParams(
            collective_id=0, has_side_effects=True, vmem_limit_bytes=48 * 2**20),
    )(conductivity, perturbation, fields, increment_start, adjoint_start, jnp.swapaxes(receivers, 1, 2), dipole_weight)


def solution(mesh):
    return jax.shard_map(
        on_device,
        mesh=mesh,
        in_specs=(
            P("gz", None, None),
            P("gz", None, None),
            P("src", "gz", None, None),
            P("src", "gz", None, None),
            P("src", "gz", None, None),
            P("src", None, None),
            P("src", None),
        ),
        out_specs=(P("gz", "src", None), P("src", "gz", None, None)),
        check_vma=False,
    )
```

time: 342 us -> 66.2 us (0.19)
  waiting for transfers between devices: 164 us -> 0 us
  blocking collectives: 68.9 us -> 0 us
  Pallas kernels: 0 us -> 57.3 us
  other arithmetic: 35.9 us -> 0 us
  starting transfers between devices: 35 us -> 0 us
  local copies, waits for them, and re-layouts: 22.9 us -> 7.8 us
  between operations: 14.8 us -> 0.66 us
    psum x1 -> x0, waiting for transfers between devices: 160 us -> none  [on_device(): summed = lax.psum(partial_corr, 'src')]
    psum x1 -> x0, blocking collectives: 68.9 us -> none  [build_adjoint_source(): reading = dipole_weight * lax.psum(partial_read, 'gz')]
    pallas_call x0 -> x1, Pallas kernels: none -> 57.3 us  [on_device(): pl.pallas_call(kernel, out_shape=(jax.ShapeDtypeStruct((depth, share, ny)...]
    ppermute x12 -> x0, starting transfers between devices: 35 us -> none  [the longest x6 27.1 us: with_halo(): before = lax.ppermute(last, axis, up)]
    gather x3 -> x0, local copies, waits for them, and re-layouts: 18.3 us -> none  [build_adjoint_source(): picked = jnp.take_along_axis(cells, safe_index.reshape(sources, -1), axis=1)]
    unnamed x7 -> x0, other arithmetic: 17.5 us -> none
    add x6 -> x0, other arithmetic: 8.41 us -> none  [the longest x2 4.62 us: on_device(): adjoint + RELAXATION * (adjoint_source - operate(sig_pad, padded)) / diag...]
    concatenate x7 -> x0, other arithmetic: 6.02 us -> none  [the longest x6 4.81 us: with_halo(): x = jnp.concatenate([before, x, after], axis=dim)]
  transfers between devices with their start and end apart: 13 -> 0, of which waited for: 5 -> 0; matrix products, arithmetic and copies ran while one was open for 4% -> 0% of each run, Pallas kernels for 0% -> 0%
where the time goes in v1:
time: 66.2 us; the launch traced here: 65.8 us
  Pallas kernels  57.3 us (87%)
  local copies, waits for them, and re-layouts  7.8 us (12%)
    pallas_call x1, Pallas kernels, on_device(): pl.pallas_call(kernel, out_shape=(jax.ShapeDtypeStruct((depth, share, ny)...  57.3 us
    unnamed x16, local copies, waits for them, and re-layouts  7.8 us

profile of v1, /device:TPU:1, one launch (start us, length us, event | category | flops | bytes accessed | tf_op | source)
XLA Modules:
  0.0 65.8 jit_solution(7544252355180218389)
XLA Ops:
  0.6 0.0 copy-start
  0.6 1.0 %copy-done = f32[2,4,128,128]{3,2,1,0:T(8,128)S(1)} copy-done((f32[2,4,128,128]{3,2,1,0:T(8,128)S(1)}, f32[2,4,128,128]{3,2,1,0:T(8,128)}, u32[]{:S(2)}) %copy-start) | copy-done | bytes 524312
  1.7 0.0 copy-start.1
  1.7 1.0 %copy-done.1 = f32[2,4,128,128]{3,2,1,0:T(8,128)S(1)} copy-done((f32[2,4,128,128]{3,2,1,0:T(8,128)S(1)}, f32[2,4,128,128]{3,2,1,0:T(8,128)}, u32[]{:S(2)}) %copy-start.1) | copy-done | bytes 524312
  2.7 0.0 copy-start.2
  2.7 1.0 %copy-done.2 = f32[2,4,128,128]{3,2,1,0:T(8,128)S(1)} copy-done((f32[2,4,128,128]{3,2,1,0:T(8,128)S(1)}, f32[2,4,128,128]{3,2,1,0:T(8,128)}, u32[]{:S(2)}) %copy-start.2) | copy-done | bytes 524312
  3.8 0.0 copy-start.3
  3.8 0.9 %copy-done.3 = f32[4,128,128]{2,1,0:T(8,128)S(1)} copy-done((f32[4,128,128]{2,1,0:T(8,128)S(1)}, f32[4,128,128]{2,1,0:T(8,128)}, u32[]{:S(2)}) %copy-start.3) | copy-done | bytes 262168
  4.7 0.0 copy-start.4
  4.7 0.9 %copy-done.4 = f32[4,128,128]{2,1,0:T(8,128)S(1)} copy-done((f32[4,128,128]{2,1,0:T(8,128)S(1)}, f32[4,128,128]{2,1,0:T(8,128)}, u32[]{:S(2)}) %copy-start.4) | copy-done | bytes 262168
  5.7 0.0 copy-start.5
  5.7 0.7 %copy-done.5 = s32[2,512,2]{1,2,0:T(2,128)S(1)} copy-done((s32[2,512,2]{1,2,0:T(2,128)S(1)}, s32[2,512,2]{1,2,0:T(2,128)}, u32[]{:S(2)}) %copy-start.5) | copy-done | bytes 8216
  6.4 0.0 copy-start.6
  6.4 0.7 %copy-done.6 = f32[2,512]{1,0:T(2,128)S(1)} copy-done((f32[2,512]{1,0:T(2,128)S(1)}, f32[2,512]{1,0:T(2,128)}, u32[]{:S(2)}) %copy-start.6) | copy-done | bytes 4120
  7.0 57.3 %shard_map.86 = (f32[4,8,128]{2,1,0:T(8,128)S(1)}, f32[2,4,128,128]{3,2,1,0:T(8,128)S(1)}) custom-call(f32[4,128,128]{2,1,0:T(8,128)S(1)} %copy-done.3, f32[4,128,128]{2,1,0:T(8,128)S(1)} %copy-done.4, f32[2,4,128,128]{3,2,1,0:T(8,128)S(1)} %copy-done, f32[2,4,128,128]{3,2,1,0:T(8,128)S(1)} %copy-done.1, f32[2,4,128,128]{3,2,1,0:T(8,128)S(1)} %copy-done.2, ...), custom_call_target="tpu_custom_call" | custom-call | tf_op jit(solution)/shard_map/pallas_call | solution.py:409
  64.4 0.6 copy.11
  65.0 0.8 %copy.12 = f32[2,4,128,128]{3,2,1,0:T(8,128)} copy(f32[2,4,128,128]{3,2,1,0:T(8,128)S(1)} %get-tuple-element.5) | data formatting | bytes 1048576
Async XLA Ops:
  0.6 1.0 %copy-start = (f32[2,4,128,128]{3,2,1,0:T(8,128)S(1)}, f32[2,4,128,128]{3,2,1,0:T(8,128)}, u32[]{:S(2)}) copy-start(f32[2,4,128,128]{3,2,1,0:T(8,128)} %field_hbm.1) | copy-start | bytes 1572868
  1.7 1.0 %copy-start.1 = (f32[2,4,128,128]{3,2,1,0:T(8,128)S(1)}, f32[2,4,128,128]{3,2,1,0:T(8,128)}, u32[]{:S(2)}) copy-start(f32[2,4,128,128]{3,2,1,0:T(8,128)} %start_hbm.1) | copy-start | bytes 1572868
  2.7 1.0 %copy-start.2 = (f32[2,4,128,128]{3,2,1,0:T(8,128)S(1)}, f32[2,4,128,128]{3,2,1,0:T(8,128)}, u32[]{:S(2)}) copy-start(f32[2,4,128,128]{3,2,1,0:T(8,128)} %adjoint_hbm.1) | copy-start | bytes 1572868
  3.8 0.9 %copy-start.3 = (f32[4,128,128]{2,1,0:T(8,128)S(1)}, f32[4,128,128]{2,1,0:T(8,128)}, u32[]{:S(2)}) copy-start(f32[4,128,128]{2,1,0:T(8,128)} %sigma_hbm.1) | copy-start | bytes 786436
  4.7 0.9 %copy-start.4 = (f32[4,128,128]{2,1,0:T(8,128)S(1)}, f32[4,128,128]{2,1,0:T(8,128)}, u32[]{:S(2)}) copy-start(f32[4,128,128]{2,1,0:T(8,128)} %pert_hbm.1) | copy-start | bytes 786436
  5.7 0.7 %copy-start.5 = (s32[2,512,2]{1,2,0:T(2,128)S(1)}, s32[2,512,2]{1,2,0:T(2,128)}, u32[]{:S(2)}) copy-start(s32[2,512,2]{1,2,0:T(2,128)} %param.12) | copy-start | bytes 24580
  6.4 0.7 %copy-start.6 = (f32[2,512]{1,0:T(2,128)S(1)}, f32[2,512]{1,0:T(2,128)}, u32[]{:S(2)}) copy-start(f32[2,512]{1,0:T(2,128)} %weight_ref.1) | copy-start | bytes 12292

commit v2 on v1

--- a/solution.py
+++ b/solution.py
@@ -13,7 +13,6 @@
 KEEP = 1.0 - RELAXATION
 MESH = pl.DeviceIdType.MESH
 DMA = pltpu.SemaphoreType.DMA
-QUARTER = 4
 
 
 def ahead(plane, axis):
@@ -25,12 +24,12 @@
 
 
 def kernel(
-    sigma_hbm, pert_hbm, field_hbm, start_hbm, adjoint_hbm, cells_ref, weight_ref,
+    sigma_hbm, pert_hbm, field_hbm, start_hbm, adjoint_hbm, cells_hbm, weight_hbm,
     hess_ref, inc_hbm,
-    sg, pe, fe, ie, i1, o2, ae, a1, a2, b1,
+    cells_ref, weight_ref, sg, pe, fe, ie, i1, i2, o2, ae, a1, a2, b1,
     coef, ew, nb, st, vh, ns, lap,
-    hot, spot, read, got_a, part, got_b, co, rb,
-    in_sem, out_sem, z_send, z_recv, a_send, a_recv, b_send, b_recv, s_send, s_recv,
+    hot, spot, read, got, co, rb,
+    in_sem, out_sem, known, z_send, z_recv, r_send, r_recv, s_send, s_recv,
 ):
     src, gz = lax.axis_index("src"), lax.axis_index("gz")
     n_src, n_gz = lax.axis_size("src"), lax.axis_size("gz")
@@ -51,25 +50,33 @@
     lo, hi = (src, gz - 1), (src, gz + 1)
     half = n_gz // 2
     x_part, z_part = gz // half, lax.rem(gz, half)
-    z_group, z_in = z_part // QUARTER, lax.rem(z_part, QUARTER)
-    groups = half // QUARTER
-    near = []
-    for dx in range(2):
-        for dz in range(QUARTER):
-            if dx or dz:
-                near.append((src, lax.rem(x_part + dx, 2) * half + z_group * QUARTER + lax.rem(z_in + dz, QUARTER)))
-    far = [(src, x_part * half + lax.rem(z_group + d, groups) * QUARTER + z_in) for d in range(1, groups)]
+
+    def at(dx, dz):
+        return (src, lax.rem(x_part + dx, 2) * half + lax.rem(z_part + dz + half, half))
+
+    steps = sorted(range(half), key=lambda dz: -min(dz, half - dz))
+    others = [at(dx, dz) for dz in steps for dx in (1, 0) if dx or dz]
     mates = [(lax.rem(src + d, n_src), gz) for d in range(1, n_src)]
 
     barrier = pltpu.get_barrier_semaphore()
 
-    def signal(device):
-        pl.semaphore_signal(barrier, inc=1, device_id=device, device_id_type=MESH)
-
-    pl.when(has_lo)(lambda: signal(lo))
-    pl.when(has_hi)(lambda: signal(hi))
-    for device in near + far + mates:
+    def signal(device, semaphore=barrier):
+        pl.semaphore_signal(semaphore, inc=1, device_id=device, device_id_type=MESH)
+
+    greeted = [at(0, 1), at(0, -1), at(1, 0), *mates]
+    joint = jnp.logical_or(gz == half - 1, gz == half)
+    for device in greeted:
         signal(device)
+    pl.when(joint)(lambda: signal((src, n_gz - 1 - gz)))
+
+    rounds = [[at(0, 1), at(0, -1)], [at(0, 2), at(0, -2)], [at(0, 4), at(0, -4)], [at(1, 0)]]
+
+    def tell(i):
+        for device in rounds[i]:
+            signal(device, known.at[i])
+
+    def meet(i):
+        pl.semaphore_wait(known.at[i], len(rounds[i]))
 
     loads = [
         pltpu.make_async_copy(sigma_hbm, sg.at[pl.ds(3, depth)], in_sem.at[0]),
@@ -77,6 +84,8 @@
         pltpu.make_async_copy(start_hbm, ie.at[:, pl.ds(1, depth)], in_sem.at[2]),
         pltpu.make_async_copy(field_hbm, fe.at[:, pl.ds(1, depth)], in_sem.at[3]),
         pltpu.make_async_copy(adjoint_hbm, ae.at[:, pl.ds(3, depth)], in_sem.at[4]),
+        pltpu.make_async_copy(cells_hbm, cells_ref, in_sem.at[5]),
+        pltpu.make_async_copy(weight_hbm, weight_ref, in_sem.at[6]),
     ]
     for load in loads:
         load.start()
@@ -128,12 +137,11 @@
 
     for load in loads:
         load.wait()
-    pl.semaphore_wait(barrier, len(near) + len(far) + len(mates) + has_lo.astype(jnp.int32) + has_hi.astype(jnp.int32))
+    pl.semaphore_wait(barrier, len(greeted) + joint.astype(jnp.int32))
 
     begin(edge_sigma)
     begin(edge_pert)
-    begin(edge_start)
-    begin(edge_field)
+    tell(0)
 
     def local(k, carry):
         below, above = jnp.maximum(k - 1, 0), jnp.minimum(k + 1, depth - 1)
@@ -154,7 +162,7 @@
                 other = neighbour(field, side)
                 term = term + weight * other
                 near_field = near_field + other
-            st[s, k] = term
+            st[s, k + 1] = term
             ns[s, k] = near_field
             total = term + sig_z[0] * ie[s, below + 1] + sig_z[1] * ie[s, above + 1]
             for side, weight in zip(sides, sig_w):
@@ -164,7 +172,8 @@
         return carry
 
     lax.fori_loop(0, depth, local, 0)
-    begin(edge_value)
+    meet(0)
+    tell(1)
 
     def electrodes(s):
         both = cells_ref[s]
@@ -189,6 +198,12 @@
 
     for s in range(sources):
         mark(s)
+    meet(1)
+    tell(2)
+    sent(edge_sigma)
+    sent(edge_pert)
+    begin(edge_field)
+    begin(edge_adj)
 
     arrived(edge_sigma)
 
@@ -217,54 +232,51 @@
             total = total + coef[i, e] * shifted(center, side)
         return center, total
 
-    sent(edge_sigma)
-    sent(edge_pert)
-    sent(edge_start)
-    sent(edge_field)
-    sent(edge_value)
-    begin(edge_adj)
+    meet(2)
+    tell(3)
     arrived(edge_pert)
-    arrived(edge_start)
-    arrived(edge_field)
-    arrived(edge_value)
+
+    faces = ((0, -1, 0), (depth - 1, depth, 1))
+
+    def face_weights(own, other):
+        return 0.5 * (sg[own + 3] + sg[other + 3]), 0.5 * (pe[own + 1] + pe[other + 1])
 
     for k in range(1, depth - 1):
         for s in range(sources):
-            i1[s, k + 1] = KEEP * ie[s, k + 1] + ew[k + 2] * nb[s, k]
-    for own, other, v in ((0, -1, 0), (depth - 1, depth, 1)):
-        sig_w = 0.5 * (sg[own + 3] + sg[other + 3])
-        pert_w = 0.5 * (pe[own + 1] + pe[other + 1])
-        lap[:, own] = lap[:, own] + (pe[own + 1] - pe[other + 1]).reshape(n_src, nx // n_src, ny)
-        for s in range(sources):
-            face = pert_w * (fe[s, other + 1] - fe[s, own + 1])
-            st[s, own] = st[s, own] + face
-            i1[s, own + 1] = KEEP * ie[s, own + 1] + ew[own + 2] * (nb[s, own] + face + sig_w * ie[s, other + 1])
-            i1[s, other + 1] = KEEP * ie[s, other + 1] + ew[other + 2] * (vh[v, s] - face + sig_w * ie[s, own + 1])
-    for k in range(depth - 1):
-        face = (pe[k + 1] - pe[k + 2]).reshape(n_src, nx // n_src, ny)
-        lap[:, k] = lap[:, k] + face
-        lap[:, k + 1] = lap[:, k + 1] - face
-
-    def second(k, carry):
-        for s in range(sources):
-            center, total = around(k + 2, i1, s, 1)
-            o2[s, k] = KEEP * center + ew[k + 2] * st[s, k] + total
-        return carry
-
-    lax.fori_loop(0, depth, second, 0)
-    store = pltpu.make_async_copy(o2, inc_hbm, out_sem)
-    store.start()
+            i1[s, k + 2] = KEEP * ie[s, k + 1] + ew[k + 2] * nb[s, k]
+    for own, other, v in faces:
+        sig_w, pert_w = face_weights(own, other)
+        for s in range(sources):
+            moved = pert_w * fe[s, own + 1]
+            st[s, own + 1] = st[s, own + 1] - moved
+            st[s, other + 1] = moved
+            i1[s, own + 2] = KEEP * ie[s, own + 1] + ew[own + 2] * (nb[s, own] - moved)
+            i1[s, other + 2] = ew[other + 2] * (sig_w * ie[s, own + 1] + moved)
+    for s in range(sources):
+        i1[s, 0] = empty
+        i1[s, depth + 3] = empty
+
+    def second(e, carry):
+        for s in range(sources):
+            center, total = around(e, i1, s, 0)
+            i2[s, e] = KEEP * center + ew[e] * st[s, e - 1] + total
+        return carry
+
+    lax.fori_loop(1, depth + 3, second, 0)
+    for s in range(sources):
+        i2[s, 0] = coef[5, 0] * i1[s, 1]
+        i2[s, depth + 3] = coef[4, depth + 3] * i1[s, depth + 2]
 
     def pick(s):
         rows, _ = electrodes(s)
-        value = o2[s].reshape(depth * nx, ny)
+        value = i2[s].reshape((depth + 4) * nx, ny)
         high = value.astype(jnp.bfloat16)
         rest = value - high.astype(jnp.float32)
         middle = rest.astype(jnp.bfloat16)
         low = (rest - middle.astype(jnp.float32)).astype(jnp.bfloat16)
         columns = jnp.dot(
             jnp.concatenate([high, middle, low], axis=1), spot[s], preferred_element_type=jnp.float32)
-        index = lax.broadcasted_iota(jnp.int32, columns.shape, 0) + 2 * nx
+        index = lax.broadcasted_iota(jnp.int32, columns.shape, 0)
         picked = jnp.sum(jnp.where(jnp.broadcast_to(rows, columns.shape) == index, columns, 0.0), axis=0, keepdims=True)
         reading = picked[:, :dipoles] - picked[:, dipoles:]
         for i in range(dipoles // 128):
@@ -282,7 +294,14 @@
             copies[-1].start()
         return copies
 
-    near_copies = spread(near, lambda i: read, got_a, a_send, a_recv)
+    meet(3)
+    read_copies = spread(others, lambda i: read, got, r_send, r_recv)
+
+    sent(edge_field)
+    sent(edge_adj)
+    begin(edge_start)
+    begin(edge_value)
+    arrived(edge_field)
 
     def across(k, carry):
         for s in range(sources):
@@ -290,13 +309,6 @@
         return carry
 
     lax.fori_loop(0, depth, across, 0)
-
-    total = read[...]
-    for i, copy in enumerate(near_copies):
-        copy.wait_recv()
-        total = total + got_a[i]
-    part[...] = total
-    far_copies = spread(far, lambda i: part, got_b, b_send, b_recv)
 
     arrived(edge_adj)
 
@@ -316,11 +328,18 @@
 
     lax.fori_loop(1, depth + 3, adjoint_second, 0)
 
-    total = part[...]
-    for i, copy in enumerate(far_copies):
+    for own, other, v in faces:
+        lap[:, own] = lap[:, own] + (pe[own + 1] - pe[other + 1]).reshape(n_src, nx // n_src, ny)
+    for k in range(depth - 1):
+        face = (pe[k + 1] - pe[k + 2]).reshape(n_src, nx // n_src, ny)
+        lap[:, k] = lap[:, k] + face
+        lap[:, k + 1] = lap[:, k + 1] - face
+
+    total = read[...]
+    for i, copy in enumerate(read_copies):
         copy.wait_recv()
-        total = total + got_b[i]
-    for copy in near_copies + far_copies:
+        total = total + got[i]
+    for copy in read_copies:
         copy.wait_send()
     read[...] = total
 
@@ -367,13 +386,36 @@
     lax.fori_loop(0, depth, correlate, 0)
 
     mate_copies = spread(mates, lambda i: co.at[mates[i][0]], rb, s_send, s_recv)
+
+    arrived(edge_start)
+    arrived(edge_value)
+    for own, other, v in faces:
+        sig_w, pert_w = face_weights(own, other)
+        for s in range(sources):
+            moved = pert_w * fe[s, other + 1]
+            start = ie[s, other + 1]
+            st[s, own + 1] = st[s, own + 1] + moved
+            i1[s, own + 2] = i1[s, own + 2] + ew[own + 2] * (moved + sig_w * start)
+            i1[s, other + 2] = i1[s, other + 2] + KEEP * start + ew[other + 2] * (vh[v, s] - moved)
+
+    def increment(k, carry):
+        for s in range(sources):
+            center, total = around(k + 2, i1, s, 0)
+            o2[s, k] = KEEP * center + ew[k + 2] * st[s, k + 1] + total
+        return carry
+
+    lax.fori_loop(0, depth, increment, 0)
+    store = pltpu.make_async_copy(o2, inc_hbm, out_sem)
+    store.start()
+
     total = co[src]
     for i, copy in enumerate(mate_copies):
         copy.wait_recv()
         total = total + rb[i]
     hess_ref[...] = REGULARIZE * lap[src] - total
 
-    sent(edge_adj)
+    sent(edge_start)
+    sent(edge_value)
     for copy in mate_copies:
         copy.wait_send()
     store.wait()
@@ -389,22 +431,22 @@
     def planes(*lead):
         return pltpu.VMEM((*lead, nx, ny), jnp.float32)
 
-    near, far, mates = 2 * QUARTER - 1, n_gz // 2 // QUARTER - 1, n_src - 1
+    others, mates = n_gz - 1, n_src - 1
     scratch = [
+        pltpu.VMEM((sources, 2, dipoles), jnp.int32), pltpu.VMEM((sources, dipoles), jnp.float32),
         planes(depth + 6), planes(depth + 2), planes(sources, depth + 2), planes(sources, depth + 2),
-        planes(sources, depth + 2), planes(sources, depth), planes(sources, depth + 6), planes(sources, depth + 4),
-        planes(sources, depth + 2), planes(sources, depth + 4),
-        planes(6, depth + 4), planes(depth + 4), planes(sources, depth), planes(sources, depth),
+        planes(sources, depth + 4), planes(sources, depth + 4), planes(sources, depth),
+        planes(sources, depth + 6), planes(sources, depth + 4), planes(sources, depth + 2), planes(sources, depth + 4),
+        planes(6, depth + 4), planes(depth + 4), planes(sources, depth), planes(sources, depth + 2),
         planes(2, sources), planes(sources, depth), pltpu.VMEM((n_src, depth, share, ny), jnp.float32),
         pltpu.VMEM((sources, (depth + 4) * nx, 2 * dipoles), jnp.bfloat16),
         pltpu.VMEM((sources, 3 * ny, 2 * dipoles), jnp.bfloat16),
-        pltpu.VMEM((rows, 128), jnp.float32), pltpu.VMEM((near, rows, 128), jnp.float32),
-        pltpu.VMEM((rows, 128), jnp.float32), pltpu.VMEM((far, rows, 128), jnp.float32),
+        pltpu.VMEM((rows, 128), jnp.float32), pltpu.VMEM((others, rows, 128), jnp.float32),
         pltpu.VMEM((n_src, depth, share, ny), jnp.float32), pltpu.VMEM((mates, depth, share, ny), jnp.float32),
-        DMA((5,)), DMA, DMA((2, 6)), DMA((2, 6)), DMA((near,)), DMA((near,)), DMA((far,)), DMA((far,)),
+        DMA((7,)), DMA, pltpu.SemaphoreType.REGULAR((4,)), DMA((2, 6)), DMA((2, 6)), DMA((others,)), DMA((others,)),
         DMA((mates,)), DMA((mates,)),
     ]
-    anywhere = pl.BlockSpec(memory_space=pl.ANY)
+    anywhere = pl.BlockSpec(memory_space=pltpu.HBM)
     vmem = pl.BlockSpec(memory_space=pltpu.VMEM)
     return pl.pallas_call(
         kernel,
@@ -412,11 +454,11 @@
             jax.ShapeDtypeStruct((depth, share, ny), jnp.float32),
             jax.ShapeDtypeStruct(increment_start.shape, jnp.float32),
         ),
-        in_specs=[anywhere] * 5 + [vmem] * 2,
+        in_specs=[anywhere] * 7,
         out_specs=(vmem, anywhere),
         scratch_shapes=scratch,
         compiler_params=pltpu.CompilerParams(
-            collective_id=0, has_side_effects=True, vmem_limit_bytes=48 * 2**20),
+            collective_id=0, has_side_effects=True, vmem_limit_bytes=63 * 2**20),
     )(conductivity, perturbation, fields, increment_start, adjoint_start, jnp.swapaxes(receivers, 1, 2), dipole_weight)
 
 

time: 66.2 us -> 57.2 us (0.86)
  local copies, waits for them, and re-layouts: 7.8 us -> 3.2 us
  Pallas kernels: 57.3 us -> 53.1 us
    unnamed x16 -> x2, local copies, waits for them, and re-layouts: 7.8 us -> 3.2 us
    pallas_call x1, Pallas kernels: 57.3 us -> 53.1 us  [on_device(): pl.pallas_call(kernel, out_shape=(jax.ShapeDtypeStruct((depth, share, ny)...]
where the time goes in v2:
time: 57.2 us; the launch traced here: 57 us
  Pallas kernels  53.1 us (93%)
  local copies, waits for them, and re-layouts  3.2 us (6%)
  between operations  0.64 us (1%)
    pallas_call x1, Pallas kernels, on_device(): pl.pallas_call(kernel, out_shape=(jax.ShapeDtypeStruct((depth, share, ny)...  53.1 us
    unnamed x2, local copies, waits for them, and re-layouts  3.2 us

profile of v2, /device:TPU:1, one launch (start us, length us, event | category | flops | bytes accessed | tf_op | source)
XLA Modules:
  0.0 57.0 jit_solution(17285101094688317596)
XLA Ops:
  0.6 53.1 %shard_map.86 = (f32[4,8,128]{2,1,0:T(8,128)}, f32[2,4,128,128]{3,2,1,0:T(8,128)}) custom-call(f32[4,128,128]{2,1,0:T(8,128)} %sigma_hbm.1, f32[4,128,128]{2,1,0:T(8,128)} %pert_hbm.1, f32[2,4,128,128]{3,2,1,0:T(8,128)} %field_hbm.1, f32[2,4,128,128]{3,2,1,0:T(8,128)} %start_hbm.1, f32[2,4,128,128]{3,2,1,0:T(8,128)} %adjoint_hbm.1, s32[2,2,512]{2,1,0:T(2,128)} %bitcast.1, ...), custom_call_target="tpu_custom_call" | custom-call | tf_op jit(solution)/shard_map/pallas_call | solution.py:451
  53.8 1.3 %copy.11 = f32[4,8,128]{2,1,0:T(8,128)} copy(f32[4,8,128]{2,1,0:T(8,128)} %get-tuple-element.4) | data formatting | bytes 32768
  55.1 1.9 %copy.12 = f32[2,4,128,128]{3,2,1,0:T(8,128)} copy(f32[2,4,128,128]{3,2,1,0:T(8,128)} %get-tuple-element.5) | data formatting | bytes 1048576

commit v3 on v2

--- a/solution.py
+++ b/solution.py
@@ -27,9 +27,9 @@
     sigma_hbm, pert_hbm, field_hbm, start_hbm, adjoint_hbm, cells_hbm, weight_hbm,
     hess_ref, inc_hbm,
     cells_ref, weight_ref, sg, pe, fe, ie, i1, i2, o2, ae, a1, a2, b1,
-    coef, ew, nb, st, vh, ns, lap,
+    coef, ew, nb, st, ih, ns, lap,
     hot, spot, read, got, co, rb,
-    in_sem, out_sem, known, z_send, z_recv, r_send, r_recv, s_send, s_recv,
+    in_sem, out_sem, known, z_send, z_recv, c_send, c_recv, r_send, r_recv, s_send, s_recv,
 ):
     src, gz = lax.axis_index("src"), lax.axis_index("gz")
     n_src, n_gz = lax.axis_size("src"), lax.axis_size("gz")
@@ -56,7 +56,12 @@
 
     steps = sorted(range(half), key=lambda dz: -min(dz, half - dz))
     others = [at(dx, dz) for dz in steps for dx in (1, 0) if dx or dz]
-    mates = [(lax.rem(src + d, n_src), gz) for d in range(1, n_src)]
+    core = lax.rem(src, 2)
+    sibling = (src + 1 - 2 * core, gz)
+    mates = []
+    for d in range(n_src // 2 - 1, -1, -1):
+        pair = lax.rem(src // 2 + d, n_src // 2) * 2
+        mates += [(pair + 1 - core, gz), (pair + core, gz)] if d else [sibling]
 
     barrier = pltpu.get_barrier_semaphore()
 
@@ -101,8 +106,8 @@
         pe[e] = empty
         for s in range(sources):
             fe[s, e] = empty
-            ie[s, e] = empty
-            vh[1 if high else 0, s] = empty
+            for i in range(2):
+                ih[1 if high else 0, s, i] = empty
 
     pl.when(jnp.logical_not(has_lo))(lambda: clear(False))
     pl.when(jnp.logical_not(has_hi))(lambda: clear(True))
@@ -128,20 +133,32 @@
         pl.when(has_lo)(pair[0].wait_recv)
         pl.when(has_hi)(pair[1].wait_recv)
 
-    edge_sigma = edge(0, sg.at[pl.ds(depth, 3)], sg.at[pl.ds(0, 3)], sg.at[pl.ds(3, 3)], sg.at[pl.ds(depth + 3, 3)])
-    edge_pert = edge(1, pe.at[depth], pe.at[0], pe.at[1], pe.at[depth + 1])
-    edge_start = edge(2, ie.at[:, depth], ie.at[:, 0], ie.at[:, 1], ie.at[:, depth + 1])
-    edge_field = edge(3, fe.at[:, depth], fe.at[:, 0], fe.at[:, 1], fe.at[:, depth + 1])
-    edge_value = edge(4, nb.at[:, depth - 1], vh.at[0], nb.at[:, 0], vh.at[1])
-    edge_adj = edge(5, ae.at[:, pl.ds(depth, 3)], ae.at[:, pl.ds(0, 3)], ae.at[:, pl.ds(3, 3)], ae.at[:, pl.ds(depth + 3, 3)])
+    rows_here = pl.ds(pl.multiple_of(core * (nx // 2), nx // 2), nx // 2)
+    low_sigma, high_sigma = sg.at[pl.ds(0, 3), rows_here], sg.at[pl.ds(depth + 3, 3), rows_here]
+    low_pert, high_pert = pe.at[0, rows_here], pe.at[depth + 1, rows_here]
+    edge_sigma = edge(0, sigma_hbm.at[pl.ds(depth - 3, 3), rows_here], low_sigma,
+                      sigma_hbm.at[pl.ds(0, 3), rows_here], high_sigma)
+    edge_pert = edge(1, pert_hbm.at[depth - 1, rows_here], low_pert, pert_hbm.at[0, rows_here], high_pert)
+    hands = []
+    for i, half_planes in enumerate((low_sigma, low_pert, high_sigma, high_pert)):
+        hands.append(pltpu.make_async_remote_copy(
+            src_ref=half_planes, dst_ref=half_planes, send_sem=c_send.at[i], recv_sem=c_recv.at[i],
+            device_id=sibling, device_id_type=MESH))
+    edge_field = edge(2, field_hbm.at[:, depth - 1], fe.at[:, 0], field_hbm.at[:, 0], fe.at[:, depth + 1])
+    edge_adj = edge(3, adjoint_hbm.at[:, pl.ds(depth - 3, 3)], ae.at[:, pl.ds(0, 3)],
+                    adjoint_hbm.at[:, pl.ds(0, 3)], ae.at[:, pl.ds(depth + 3, 3)])
+    edge_inc = edge(4, i2.at[:, pl.ds(depth + 2, 2)], ih.at[0], i2.at[:, pl.ds(0, 2)], ih.at[1])
+
+    pl.semaphore_wait(barrier, len(greeted) + joint.astype(jnp.int32))
+
+    begin(edge_sigma)
+    begin(edge_pert)
+    begin(edge_field)
+    begin(edge_adj)
+    tell(0)
 
     for load in loads:
         load.wait()
-    pl.semaphore_wait(barrier, len(greeted) + joint.astype(jnp.int32))
-
-    begin(edge_sigma)
-    begin(edge_pert)
-    tell(0)
 
     def local(k, carry):
         below, above = jnp.maximum(k - 1, 0), jnp.minimum(k + 1, depth - 1)
@@ -200,12 +217,23 @@
         mark(s)
     meet(1)
     tell(2)
-    sent(edge_sigma)
-    sent(edge_pert)
-    begin(edge_field)
-    begin(edge_adj)
-
-    arrived(edge_sigma)
+
+    def hand_on(side):
+        edge_sigma[side].wait_recv()
+        hands[2 * side].start()
+        edge_pert[side].wait_recv()
+        hands[2 * side + 1].start()
+
+    def handed(side):
+        for hand in hands[2 * side:2 * side + 2]:
+            hand.wait()
+
+    pl.when(has_lo)(lambda: hand_on(0))
+    pl.when(has_hi)(lambda: hand_on(1))
+    meet(2)
+    tell(3)
+    pl.when(has_lo)(lambda: handed(0))
+    pl.when(has_hi)(lambda: handed(1))
 
     def coefficients(e, carry):
         sig, below, above = sg[e + 1], sg[e], sg[e + 2]
@@ -232,11 +260,7 @@
             total = total + coef[i, e] * shifted(center, side)
         return center, total
 
-    meet(2)
-    tell(3)
-    arrived(edge_pert)
-
-    faces = ((0, -1, 0), (depth - 1, depth, 1))
+    faces = ((0, -1), (depth - 1, depth))
 
     def face_weights(own, other):
         return 0.5 * (sg[own + 3] + sg[other + 3]), 0.5 * (pe[own + 1] + pe[other + 1])
@@ -244,7 +268,7 @@
     for k in range(1, depth - 1):
         for s in range(sources):
             i1[s, k + 2] = KEEP * ie[s, k + 1] + ew[k + 2] * nb[s, k]
-    for own, other, v in faces:
+    for own, other in faces:
         sig_w, pert_w = face_weights(own, other)
         for s in range(sources):
             moved = pert_w * fe[s, own + 1]
@@ -297,10 +321,10 @@
     meet(3)
     read_copies = spread(others, lambda i: read, got, r_send, r_recv)
 
+    sent(edge_sigma)
+    sent(edge_pert)
     sent(edge_field)
     sent(edge_adj)
-    begin(edge_start)
-    begin(edge_value)
     arrived(edge_field)
 
     def across(k, carry):
@@ -311,6 +335,7 @@
     lax.fori_loop(0, depth, across, 0)
 
     arrived(edge_adj)
+    begin(edge_inc)
 
     def adjoint_first(e, carry):
         for s in range(sources):
@@ -328,7 +353,7 @@
 
     lax.fori_loop(1, depth + 3, adjoint_second, 0)
 
-    for own, other, v in faces:
+    for own, other in faces:
         lap[:, own] = lap[:, own] + (pe[own + 1] - pe[other + 1]).reshape(n_src, nx // n_src, ny)
     for k in range(depth - 1):
         face = (pe[k + 1] - pe[k + 2]).reshape(n_src, nx // n_src, ny)
@@ -387,24 +412,10 @@
 
     mate_copies = spread(mates, lambda i: co.at[mates[i][0]], rb, s_send, s_recv)
 
-    arrived(edge_start)
-    arrived(edge_value)
-    for own, other, v in faces:
-        sig_w, pert_w = face_weights(own, other)
-        for s in range(sources):
-            moved = pert_w * fe[s, other + 1]
-            start = ie[s, other + 1]
-            st[s, own + 1] = st[s, own + 1] + moved
-            i1[s, own + 2] = i1[s, own + 2] + ew[own + 2] * (moved + sig_w * start)
-            i1[s, other + 2] = i1[s, other + 2] + KEEP * start + ew[other + 2] * (vh[v, s] - moved)
-
-    def increment(k, carry):
-        for s in range(sources):
-            center, total = around(k + 2, i1, s, 0)
-            o2[s, k] = KEEP * center + ew[k + 2] * st[s, k + 1] + total
-        return carry
-
-    lax.fori_loop(0, depth, increment, 0)
+    arrived(edge_inc)
+    for s in range(sources):
+        for k in range(depth):
+            o2[s, k] = i2[s, k + 2] + (ih[0, s, k] if k < 2 else ih[1, s, k + 2 - depth])
     store = pltpu.make_async_copy(o2, inc_hbm, out_sem)
     store.start()
 
@@ -414,8 +425,7 @@
         total = total + rb[i]
     hess_ref[...] = REGULARIZE * lap[src] - total
 
-    sent(edge_start)
-    sent(edge_value)
+    sent(edge_inc)
     for copy in mate_copies:
         copy.wait_send()
     store.wait()
@@ -438,12 +448,12 @@
         planes(sources, depth + 4), planes(sources, depth + 4), planes(sources, depth),
         planes(sources, depth + 6), planes(sources, depth + 4), planes(sources, depth + 2), planes(sources, depth + 4),
         planes(6, depth + 4), planes(depth + 4), planes(sources, depth), planes(sources, depth + 2),
-        planes(2, sources), planes(sources, depth), pltpu.VMEM((n_src, depth, share, ny), jnp.float32),
+        planes(2, sources, 2), planes(sources, depth), pltpu.VMEM((n_src, depth, share, ny), jnp.float32),
         pltpu.VMEM((sources, (depth + 4) * nx, 2 * dipoles), jnp.bfloat16),
         pltpu.VMEM((sources, 3 * ny, 2 * dipoles), jnp.bfloat16),
         pltpu.VMEM((rows, 128), jnp.float32), pltpu.VMEM((others, rows, 128), jnp.float32),
         pltpu.VMEM((n_src, depth, share, ny), jnp.float32), pltpu.VMEM((mates, depth, share, ny), jnp.float32),
-        DMA((7,)), DMA, pltpu.SemaphoreType.REGULAR((4,)), DMA((2, 6)), DMA((2, 6)), DMA((others,)), DMA((others,)),
+        DMA((7,)), DMA, pltpu.SemaphoreType.REGULAR((4,)), DMA((2, 5)), DMA((2, 5)), DMA((4,)), DMA((4,)), DMA((others,)), DMA((others,)),
         DMA((mates,)), DMA((mates,)),
     ]
     anywhere = pl.BlockSpec(memory_space=pltpu.HBM)

time: 57.2 us -> 53.8 us (0.941)
  Pallas kernels: 53.1 us -> 49.7 us
    pallas_call x1, Pallas kernels: 53.1 us -> 49.7 us  [on_device(): pl.pallas_call(kernel, out_shape=(jax.ShapeDtypeStruct((depth, share, ny)...]
where the time goes in v3:
time: 53.8 us; the launch traced here: 53.6 us
  Pallas kernels  49.7 us (92%)
  local copies, waits for them, and re-layouts  3.2 us (6%)
  between operations  0.64 us (1%)
    pallas_call x1, Pallas kernels, on_device(): pl.pallas_call(kernel, out_shape=(jax.ShapeDtypeStruct((depth, share, ny)...  49.7 us
    unnamed x2, local copies, waits for them, and re-layouts  3.2 us

profile of v3, /device:TPU:1, one launch (start us, length us, event | category | flops | bytes accessed | tf_op | source)
XLA Modules:
  0.0 53.6 jit_solution(7065870766844476361)
XLA Ops:
  0.6 49.7 %shard_map.86 = (f32[4,8,128]{2,1,0:T(8,128)}, f32[2,4,128,128]{3,2,1,0:T(8,128)}) custom-call(f32[4,128,128]{2,1,0:T(8,128)} %sigma_hbm.1, f32[4,128,128]{2,1,0:T(8,128)} %pert_hbm.1, f32[2,4,128,128]{3,2,1,0:T(8,128)} %field_hbm.1, f32[2,4,128,128]{3,2,1,0:T(8,128)} %start_hbm.1, f32[2,4,128,128]{3,2,1,0:T(8,128)} %adjoint_hbm.1, s32[2,2,512]{2,1,0:T(2,128)} %bitcast.1, ...), custom_call_target="tpu_custom_call" | custom-call | tf_op jit(solution)/shard_map/pallas_call | solution.py:461
  50.4 1.3 %copy.11 = f32[4,8,128]{2,1,0:T(8,128)} copy(f32[4,8,128]{2,1,0:T(8,128)} %get-tuple-element.4) | data formatting | bytes 32768
  51.7 1.9 %copy.12 = f32[2,4,128,128]{3,2,1,0:T(8,128)} copy(f32[2,4,128,128]{3,2,1,0:T(8,128)} %get-tuple-element.5) | data formatting | bytes 1048576

commit v4 on v3

--- a/solution.py
+++ b/solution.py
@@ -153,8 +153,8 @@
 
     begin(edge_sigma)
     begin(edge_pert)
+    begin(edge_adj)
     begin(edge_field)
-    begin(edge_adj)
     tell(0)
 
     for load in loads:
@@ -321,18 +321,6 @@
     meet(3)
     read_copies = spread(others, lambda i: read, got, r_send, r_recv)
 
-    sent(edge_sigma)
-    sent(edge_pert)
-    sent(edge_field)
-    sent(edge_adj)
-    arrived(edge_field)
-
-    def across(k, carry):
-        for s in range(sources):
-            ns[s, k] = ns[s, k] + (fe[s, k] + fe[s, k + 2])
-        return carry
-
-    lax.fori_loop(0, depth, across, 0)
 
     arrived(edge_adj)
     begin(edge_inc)
@@ -389,6 +377,15 @@
         return carry
 
     lax.fori_loop(1, depth + 3, adjoint_readings, 0)
+
+    arrived(edge_field)
+
+    def across(k, carry):
+        for s in range(sources):
+            ns[s, k] = ns[s, k] + (fe[s, k] + fe[s, k + 2])
+        return carry
+
+    lax.fori_loop(0, depth, across, 0)
 
     def correlate(k, carry):
         product = empty
@@ -425,7 +422,8 @@
         total = total + rb[i]
     hess_ref[...] = REGULARIZE * lap[src] - total
 
-    sent(edge_inc)
+    for pair in (edge_sigma, edge_pert, edge_adj, edge_field, edge_inc):
+        sent(pair)
     for copy in mate_copies:
         copy.wait_send()
     store.wait()

time: 53.8 us -> 53.4 us (level)
  no operation moved by 1% of the time
where the time goes in v4:
time: 53.4 us; the launch traced here: 53.2 us
  Pallas kernels  49.4 us (93%)
  local copies, waits for them, and re-layouts  3.2 us (6%)
  between operations  0.64 us (1%)
    pallas_call x1, Pallas kernels, on_device(): pl.pallas_call(kernel, out_shape=(jax.ShapeDtypeStruct((depth, share, ny)...  49.4 us
    unnamed x2, local copies, waits for them, and re-layouts  3.2 us

profile of v4, /device:TPU:1, one launch (start us, length us, event | category | flops | bytes accessed | tf_op | source)
XLA Modules:
  0.0 53.2 jit_solution(11735837545558335797)
XLA Ops:
  0.6 49.4 %shard_map.86 = (f32[4,8,128]{2,1,0:T(8,128)}, f32[2,4,128,128]{3,2,1,0:T(8,128)}) custom-call(f32[4,128,128]{2,1,0:T(8,128)} %sigma_hbm.1, f32[4,128,128]{2,1,0:T(8,128)} %pert_hbm.1, f32[2,4,128,128]{3,2,1,0:T(8,128)} %field_hbm.1, f32[2,4,128,128]{3,2,1,0:T(8,128)} %start_hbm.1, f32[2,4,128,128]{3,2,1,0:T(8,128)} %adjoint_hbm.1, s32[2,2,512]{2,1,0:T(2,128)} %bitcast.1, ...), custom_call_target="tpu_custom_call" | custom-call | tf_op jit(solution)/shard_map/pallas_call | solution.py:459
  50.0 1.3 %copy.11 = f32[4,8,128]{2,1,0:T(8,128)} copy(f32[4,8,128]{2,1,0:T(8,128)} %get-tuple-element.4) | data formatting | bytes 32768
  51.3 1.9 %copy.12 = f32[2,4,128,128]{3,2,1,0:T(8,128)} copy(f32[2,4,128,128]{3,2,1,0:T(8,128)} %get-tuple-element.5) | data formatting | bytes 1048576

commit v5 on v4

--- a/solution.py
+++ b/solution.py
@@ -28,8 +28,8 @@
     hess_ref, inc_hbm,
     cells_ref, weight_ref, sg, pe, fe, ie, i1, i2, o2, ae, a1, a2, b1,
     coef, ew, nb, st, ih, ns, lap,
-    hot, spot, read, got, co, rb,
-    in_sem, out_sem, known, z_send, z_recv, c_send, c_recv, r_send, r_recv, s_send, s_recv,
+    hot, spot, read, got_pair, part, got, co, rb,
+    in_sem, out_sem, known, z_send, z_recv, c_send, c_recv, p_send, p_recv, r_send, r_recv, s_send, s_recv,
 ):
     src, gz = lax.axis_index("src"), lax.axis_index("gz")
     n_src, n_gz = lax.axis_size("src"), lax.axis_size("gz")
@@ -55,7 +55,7 @@
         return (src, lax.rem(x_part + dx, 2) * half + lax.rem(z_part + dz + half, half))
 
     steps = sorted(range(half), key=lambda dz: -min(dz, half - dz))
-    others = [at(dx, dz) for dz in steps for dx in (1, 0) if dx or dz]
+    ring = [at(0, dz) for dz in steps if dz]
     core = lax.rem(src, 2)
     sibling = (src + 1 - 2 * core, gz)
     mates = []
@@ -74,7 +74,7 @@
         signal(device)
     pl.when(joint)(lambda: signal((src, n_gz - 1 - gz)))
 
-    rounds = [[at(0, 1), at(0, -1)], [at(0, 2), at(0, -2)], [at(0, 4), at(0, -4)], [at(1, 0)]]
+    rounds = [[at(0, 1), at(0, -1)], [at(0, 2), at(0, -2)], [at(0, 4), at(0, -4)]]
 
     def tell(i):
         for device in rounds[i]:
@@ -231,7 +231,6 @@
     pl.when(has_lo)(lambda: hand_on(0))
     pl.when(has_hi)(lambda: hand_on(1))
     meet(2)
-    tell(3)
     pl.when(has_lo)(lambda: handed(0))
     pl.when(has_hi)(lambda: handed(1))
 
@@ -318,9 +317,10 @@
             copies[-1].start()
         return copies
 
-    meet(3)
-    read_copies = spread(others, lambda i: read, got, r_send, r_recv)
-
+    pair_copies = spread([at(1, 0)], lambda i: read, got_pair, p_send, p_recv)
+    pair_copies[0].wait_recv()
+    part[...] = read[...] + got_pair[0]
+    read_copies = spread(ring, lambda i: part, got, r_send, r_recv)
 
     arrived(edge_adj)
     begin(edge_inc)
@@ -348,11 +348,11 @@
         lap[:, k] = lap[:, k] + face
         lap[:, k + 1] = lap[:, k + 1] - face
 
-    total = read[...]
+    total = part[...]
     for i, copy in enumerate(read_copies):
         copy.wait_recv()
         total = total + got[i]
-    for copy in read_copies:
+    for copy in pair_copies + read_copies:
         copy.wait_send()
     read[...] = total
 
@@ -439,7 +439,7 @@
     def planes(*lead):
         return pltpu.VMEM((*lead, nx, ny), jnp.float32)
 
-    others, mates = n_gz - 1, n_src - 1
+    others, mates = n_gz // 2 - 1, n_src - 1
     scratch = [
         pltpu.VMEM((sources, 2, dipoles), jnp.int32), pltpu.VMEM((sources, dipoles), jnp.float32),
         planes(depth + 6), planes(depth + 2), planes(sources, depth + 2), planes(sources, depth + 2),
@@ -449,9 +449,10 @@
         planes(2, sources, 2), planes(sources, depth), pltpu.VMEM((n_src, depth, share, ny), jnp.float32),
         pltpu.VMEM((sources, (depth + 4) * nx, 2 * dipoles), jnp.bfloat16),
         pltpu.VMEM((sources, 3 * ny, 2 * dipoles), jnp.bfloat16),
+        pltpu.VMEM((rows, 128), jnp.float32), pltpu.VMEM((1, rows, 128), jnp.float32),
         pltpu.VMEM((rows, 128), jnp.float32), pltpu.VMEM((others, rows, 128), jnp.float32),
         pltpu.VMEM((n_src, depth, share, ny), jnp.float32), pltpu.VMEM((mates, depth, share, ny), jnp.float32),
-        DMA((7,)), DMA, pltpu.SemaphoreType.REGULAR((4,)), DMA((2, 5)), DMA((2, 5)), DMA((4,)), DMA((4,)), DMA((others,)), DMA((others,)),
+        DMA((7,)), DMA, pltpu.SemaphoreType.REGULAR((3,)), DMA((2, 5)), DMA((2, 5)), DMA((4,)), DMA((4,)), DMA((1,)), DMA((1,)), DMA((others,)), DMA((others,)),
         DMA((mates,)), DMA((mates,)),
     ]
     anywhere = pl.BlockSpec(memory_space=pltpu.HBM)

time: 53.4 us -> 50 us (0.936)
  Pallas kernels: 49.4 us -> 45.9 us
    pallas_call x1, Pallas kernels: 49.4 us -> 45.9 us  [on_device(): pl.pallas_call(kernel, out_shape=(jax.ShapeDtypeStruct((depth, share, ny)...]
where the time goes in v5:
time: 50 us; the launch traced here: 49.8 us
  Pallas kernels  45.9 us (92%)
  local copies, waits for them, and re-layouts  3.2 us (6%)
  between operations  0.64 us (1%)
    pallas_call x1, Pallas kernels, on_device(): pl.pallas_call(kernel, out_shape=(jax.ShapeDtypeStruct((depth, share, ny)...  45.9 us
    unnamed x2, local copies, waits for them, and re-layouts  3.2 us

profile of v5, /device:TPU:1, one launch (start us, length us, event | category | flops | bytes accessed | tf_op | source)
XLA Modules:
  0.0 49.8 jit_solution(4152662496438980256)
XLA Ops:
  0.6 45.9 %shard_map.86 = (f32[4,8,128]{2,1,0:T(8,128)}, f32[2,4,128,128]{3,2,1,0:T(8,128)}) custom-call(f32[4,128,128]{2,1,0:T(8,128)} %sigma_hbm.1, f32[4,128,128]{2,1,0:T(8,128)} %pert_hbm.1, f32[2,4,128,128]{3,2,1,0:T(8,128)} %field_hbm.1, f32[2,4,128,128]{3,2,1,0:T(8,128)} %start_hbm.1, f32[2,4,128,128]{3,2,1,0:T(8,128)} %adjoint_hbm.1, s32[2,2,512]{2,1,0:T(2,128)} %bitcast.1, ...), custom_call_target="tpu_custom_call" | custom-call | tf_op jit(solution)/shard_map/pallas_call | solution.py:460
  46.6 1.3 %copy.11 = f32[4,8,128]{2,1,0:T(8,128)} copy(f32[4,8,128]{2,1,0:T(8,128)} %get-tuple-element.4) | data formatting | bytes 32768
  47.9 1.9 %copy.12 = f32[2,4,128,128]{3,2,1,0:T(8,128)} copy(f32[2,4,128,128]{3,2,1,0:T(8,128)} %get-tuple-element.5) | data formatting | bytes 1048576
